TPU v7x, 256 devices: a whole 4x4x8 slice. The times are simulated.
256 devices in a mesh: img: 4 (over x_lo, core), prm: 64 (over x_hi, y, z).
Axes of the slice: x: 4 (x_hi: 2, x_lo: 2; x = x_hi * 2 + x_lo), y: 4, z: 8, core: 2. Of those that a mesh axis runs over, the one named last changes fastest.
Arguments:
- teacher_maps: bfloat16 [16, 1024, 1152], P('img', 'prm'), may hold values from -6 to 6
- pool_index: int32 [256, 4], replicated, may hold values from 0 to 1023, as said below
- pairing: int32 [16], P('img'), may hold values from 0 to 15, as said below
- teacher_prompts: bfloat16 [32768, 1152], P('prm')
- student_patches: bfloat16 [16, 256, 768], P('img'), may hold values from -9 to 9
- student_prompts: bfloat16 [32768, 768], P('prm')
Outputs:
- patch_kl: float32 [16, 256], P('img')
- patch_grad: bfloat16 [16, 256, 768], P('img')
Inputs may be any that keep to these rules, and one draw needn't show every extreme that they name: pool_index[q, j] = r * 32 + c with grid row r within 2 * (q // 16) - 1 to 2 * (q // 16) + 2 and grid column c within 2 * (q % 16) - 1 to 2 * (q % 16) + 2, both inside the grid. `pairing`: a permutation of the 16 images.
All inputs are finite; a program needn't handle non-finite values.
Results may differ from a plain program's by a relative error of at most 0.001.
The roundings to bfloat16 on the way count: a program that leaves them out, or rounds other values in their place, can miss the bound.
Values may be sent and summed in bfloat16 or wider, within the bound.
No kernel may reach another device: no remote copies, remote signals or barrier semaphores. Data moves between devices by JAX's collectives and lax.ppermute only.
A program may use at most 64 MiB of HBM per device.

v0:
```python
import functools

import jax
import jax.numpy as jnp
from jax import lax
from jax.experimental import pallas as pl
from jax.experimental.pallas import tpu as pltpu
from jax.sharding import Mesh, PartitionSpec as P

IMG = ("xlo", "core")
PRM = ("xhi", "y", "zh", "zl")
Z = ("zh", "zl")
F32 = jnp.float32
BF16 = jnp.bfloat16
D_T = 1152
D_S = 768
PIECE = 256
ROWS = 256
CONTRACT_LAST = (((1,), (1,)), ((), ()))
CONTRACT_FIRST = (((0,), (0,)), ((), ()))


def swap(x, axis):
    return lax.all_to_all(x, axis, split_axis=0, concat_axis=0, tiled=True)


def spread(x, axis, size):
    return swap(jnp.broadcast_to(x[None], (size,) + x.shape), axis)


def exchange_sum(x, axis, starts):
    rows = x.shape[0] // 4
    total = lax.dynamic_slice_in_dim(x, starts[0], rows, 0, allow_negative_indices=False)
    for k in range(1, 4):
        part = lax.dynamic_slice_in_dim(x, starts[k], rows, 0, allow_negative_indices=False)
        total = total + lax.ppermute(part, axis, [(i, i ^ k) for i in range(4)])
    return total


def half_kernel(teacher, student, half, sems):
    rows = pl.ds(lax.axis_index("core") * PIECE, PIECE)
    copies = [
        pltpu.make_async_copy(teacher.at[rows], half.at[:, 0:D_T], sems.at[0]),
        pltpu.make_async_copy(student.at[rows], half.at[:, D_T : D_T + D_S], sems.at[1]),
    ]
    for c in copies:
        c.start()
    for c in copies:
        c.wait()


def core_half(teacher, student):
    hbm = pl.BlockSpec(memory_space=pltpu.HBM)
    return pl.pallas_call(
        half_kernel,
        in_specs=[hbm, hbm],
        out_specs=pl.BlockSpec(memory_space=pltpu.VMEM),
        out_shape=pltpu.VMEM((PIECE, D_T + D_S), BF16),
        scratch_shapes=[pltpu.SemaphoreType.DMA((2,))],
        name="half",
    )(teacher, student)


def student_kernel(student_rows, own_s, *refs):
    got, (out, total, student, prompts, logits, sems) = refs[:6], refs[6:]
    copies = []

    def copy(source, target):
        copies.append(pltpu.make_async_copy(source, target, sems.at[len(copies)]))
        copies[-1].start()

    copy(student_rows, student)
    copy(own_s, prompts.at[0 : 2 * PIECE])
    for i, piece in enumerate(got):
        at = (2 + i) * PIECE
        copy(piece.at[:, D_T : D_T + D_S], prompts.at[at : at + PIECE])
    spans = [(0, 2 * PIECE, copies[:2]), (2 * PIECE, 8 * PIECE, copies[2:])]
    sent = len(copies)
    scores = []
    for first, last, needed in spans:
        for c in needed:
            c.wait()
        scores.append(
            lax.dot_general(
                prompts[first:last], student[...], CONTRACT_LAST, preferred_element_type=F32
            )
        )
        logits[first:last] = scores[-1]
        copy(logits.at[first:last], out.at[first:last])
    top = functools.reduce(jnp.maximum, [jnp.max(x, axis=0, keepdims=True) for x in scores])
    sums = sum(jnp.sum(jnp.exp(x - top), axis=0, keepdims=True) for x in scores)
    zero = jnp.zeros_like(top)
    for i, v in enumerate((top, sums) + (zero,) * 6):
        total[i : i + 1] = v
    for c in copies[sent:]:
        c.wait()


def student_score(student, own_s, got):
    hbm = pl.BlockSpec(memory_space=pltpu.HBM)
    in_hbm = [pltpu.with_memory_space_constraint(x, pltpu.HBM) for x in (student, own_s, *got)]
    return pl.pallas_call(
        student_kernel,
        in_specs=[hbm] * 8,
        out_specs=[hbm, pl.BlockSpec(memory_space=pltpu.VMEM)],
        out_shape=[
            pltpu.HBM((8 * PIECE, ROWS), F32),
            jax.ShapeDtypeStruct((8, ROWS), F32),
        ],
        scratch_shapes=[
            pltpu.VMEM((ROWS, D_S), BF16),
            pltpu.VMEM((8 * PIECE, D_S), BF16),
            pltpu.VMEM((8 * PIECE, ROWS), F32),
            pltpu.SemaphoreType.DMA((10,)),
        ],
        compiler_params=pltpu.CompilerParams(vmem_limit_bytes=24 << 20),
        cost_estimate=pl.CostEstimate(
            flops=2 * 8 * PIECE * ROWS * D_S, bytes_accessed=6 << 20, transcendentals=0
        ),
        name="student",
    )(*in_hbm)


def teacher_kernel(pooled, total_s, own_t, scores_s, own_s, *refs):
    got, (exp_t, exp_s, prompts, total, teacher, student, sems) = refs[:6], refs[6:]
    copies = []

    def copy(source, target):
        copies.append(pltpu.make_async_copy(source, target, sems.at[len(copies)]))
        copies[-1].start()

    copy(own_t, teacher.at[0 : 2 * PIECE])
    for i, piece in enumerate(got):
        at = (2 + i) * PIECE
        copy(piece.at[:, 0:D_T], teacher.at[at : at + PIECE])
    copy(scores_s, student)
    copy(own_s, prompts.at[0 : 2 * PIECE])
    for i, piece in enumerate(got):
        at = (2 + i) * PIECE
        copy(piece.at[:, D_T : D_T + D_S], prompts.at[at : at + PIECE])

    spans = [(0, 2 * PIECE, copies[:1]), (2 * PIECE, 8 * PIECE, copies[1:7])]
    logits = []
    for first, last, needed in spans:
        for c in needed:
            c.wait()
        logits.append(
            lax.dot_general(
                teacher[first:last], pooled[...], CONTRACT_LAST, preferred_element_type=F32
            )
        )
    max_t = functools.reduce(jnp.maximum, [jnp.max(x, axis=0, keepdims=True) for x in logits])
    copies[7].wait()
    max_s, sum_s = total_s[0:1], total_s[1:2]
    sum_t = number = 0.0
    for (first, last, _), scores in zip(spans, logits):
        e_t = jnp.exp(scores - max_t)
        exp_t[first:last] = e_t
        sum_t += jnp.sum(e_t, axis=0, keepdims=True)
        number += jnp.sum(e_t * (scores - student[first:last]), axis=0, keepdims=True)
        exp_s[first:last] = jnp.exp(student[first:last] - max_s)
    zero = jnp.zeros_like(max_t)
    for i, v in enumerate((max_t, max_t, max_s, zero, sum_t, number, sum_s, zero)):
        total[i : i + 1] = v
    for c in copies[8:]:
        c.wait()


def teacher_score(pooled, scores_s, total_s, own_t, own_s, got):
    vmem = pl.BlockSpec(memory_space=pltpu.VMEM)
    hbm = pl.BlockSpec(memory_space=pltpu.HBM)
    in_hbm = [
        pltpu.with_memory_space_constraint(x, pltpu.HBM)
        for x in (own_t, scores_s, own_s, *got)
    ]
    return pl.pallas_call(
        teacher_kernel,
        in_specs=[vmem, vmem] + [hbm] * 9,
        out_specs=[vmem] * 4,
        out_shape=[
            jax.ShapeDtypeStruct((8 * PIECE, ROWS), F32),
            jax.ShapeDtypeStruct((8 * PIECE, ROWS), F32),
            jax.ShapeDtypeStruct((8 * PIECE, D_S), BF16),
            jax.ShapeDtypeStruct((8, ROWS), F32),
        ],
        scratch_shapes=[
            pltpu.VMEM((8 * PIECE, D_T), BF16),
            pltpu.VMEM((8 * PIECE, ROWS), F32),
            pltpu.SemaphoreType.DMA((15,)),
        ],
        compiler_params=pltpu.CompilerParams(vmem_limit_bytes=24 << 20),
        cost_estimate=pl.CostEstimate(
            flops=2 * 8 * PIECE * ROWS * D_T, bytes_accessed=14 << 20, transcendentals=0
        ),
        name="teacher",
    )(pooled, total_s, *in_hbm)


def grad_kernel(exp_t, exp_s, mine, stats, prompts, grad, kl):
    every = stats[...]
    top = jnp.max(every, axis=0)
    weight = pltpu.roll(jnp.exp(every - top[None]), 4, 1)
    total = jnp.sum(every * weight, axis=0)
    top_t, top_s = top[0:1], top[2:3]
    sum_t, number, sum_s = total[4:5], total[5:6], total[6:7]
    rows = number / sum_t - top_t - jnp.log(sum_t) + top_s + jnp.log(sum_s)
    rows = jnp.broadcast_to(rows, (8, ROWS))
    image = lax.broadcasted_iota(jnp.int32, rows.shape, 0)
    lane = lax.broadcasted_iota(jnp.int32, rows.shape, 1)
    placed = jnp.zeros_like(rows)
    for i in range(4):
        for y in range(4):
            moved = pltpu.roll(rows, (32 * y - 64 * y - 16 * i) % ROWS, 1)
            here = (image == i) & (lane >= 32 * y) & (lane < 32 * y + 16)
            placed = jnp.where(here, moved, placed)
    first = lax.axis_index("xhi") * 128 + lax.axis_index("zl") * 16
    kl[...] = pltpu.roll(placed, first, 1)[0:4]
    scale_t = jnp.exp(mine[0:1] - top_t) / sum_t
    scale_s = jnp.exp(mine[2:3] - top_s) / sum_s
    difference = (exp_s[...] * scale_s - exp_t[...] * scale_t).astype(BF16)
    grad[...] = lax.dot_general(
        difference, prompts[...], CONTRACT_FIRST, preferred_element_type=F32
    )


def gradient(exp_t, exp_s, mine, stats, prompts):
    vmem = pl.BlockSpec(memory_space=pltpu.VMEM)
    return pl.pallas_call(
        grad_kernel,
        in_specs=[vmem] * 5,
        out_specs=[vmem] * 2,
        out_shape=[
            jax.ShapeDtypeStruct((ROWS, D_S), F32),
            jax.ShapeDtypeStruct((4, ROWS), F32),
        ],
        compiler_params=pltpu.CompilerParams(vmem_limit_bytes=24 << 20),
        cost_estimate=pl.CostEstimate(
            flops=2 * 8 * PIECE * ROWS * D_S, bytes_accessed=8 << 20, transcendentals=0
        ),
        name="gradient",
    )(exp_t, exp_s, mine, stats, prompts)


def body(teacher_maps, pool_index, pairing, teacher_prompts, student_patches, student_prompts):
    n_w, n_z = 8, 8
    xhi, y, zh, zl = (lax.axis_index(a) for a in PRM)
    w = xhi * 4 + y
    z = zh * 2 + zl

    half = core_half(teacher_prompts, student_prompts)
    flip2, flip4 = ([(i, n - 1 - i) for i in range(n)] for n in (2, 4))
    teacher_maps, half = lax.optimization_barrier((teacher_maps, half))
    got_z = lax.ppermute(half, "zl", flip2)
    got_x = lax.ppermute(half, ("xlo", "xhi"), flip4)

    patches = student_patches.reshape(4, 2, 4, 2, 16, D_S)
    patches = lax.dynamic_index_in_dim(patches, xhi, 1, keepdims=False)
    patches = lax.dynamic_index_in_dim(patches, zl, 2, keepdims=False)
    student_rows = patches.transpose(1, 0, 2, 3).reshape(ROWS, D_S)

    source = jnp.arange(8)
    grid_row = 4 * w + source // 2
    grid_row = jnp.where(
        zl == 0,
        jnp.where(source >= 6, 4 * w - 1, grid_row),
        jnp.where(source <= 1, 4 * w + 4, grid_row),
    )
    cell_id = grid_row[:, None] * 32 + (source % 2)[:, None] * 16 + jnp.arange(16)[None]
    cell_id = cell_id.reshape(-1)
    index = lax.dynamic_slice_in_dim(pool_index, 16 * (2 * w + zl), 16, 0)
    counts = jnp.sum((index[:, :, None] == cell_id[None, None, :]).astype(F32), axis=1).astype(BF16)
    starts_y = [(y ^ k) * 64 for k in range(4)]
    starts_z = [(zh ^ k) * 16 for k in range(4)]

    every_map = lax.all_gather(teacher_maps, IMG, axis=0, tiled=True)
    wanted = pairing[:, None] == jnp.arange(16)[None]
    owned = jnp.sum(jnp.where(wanted[:, :, None, None], every_map[None], 0), axis=1, dtype=BF16)
    pairs = [((v + 1) * n_z + c, v * n_z + c) for v in range(n_w - 1) for c in (0, 1)]
    pairs += [(v * n_z + c, (v + 1) * n_z + c) for v in range(n_w - 1) for c in (6, 7)]
    halo = lax.ppermute(owned, PRM, pairs)
    lower = jnp.arange(2)[None, :, None, None] == 1
    outside = jnp.where(lower, z <= 1, z >= 6)
    to_z = jnp.where(outside, halo[:, None], owned[:, None]).reshape((8,) + owned.shape[1:])
    to_z, got_z, counts, starts_y, starts_z = lax.optimization_barrier(
        (to_z, got_z, counts, starts_y, starts_z)
    )
    got_xz = lax.ppermute(got_z, ("xlo", "xhi"), flip4)
    cells = swap(to_z, Z)
    cells = cells.reshape(128, D_T)
    pooled = (jnp.dot(counts, cells, preferred_element_type=F32) * 0.25).astype(BF16)

    pooled, got_x = lax.optimization_barrier((pooled, got_x))
    got = [got_x, got_z, got_xz]
    got += [lax.ppermute(piece, "core", flip2) for piece in got]
    scores_s, total_s = student_score(student_rows, student_prompts, got)
    pooled = spread(pooled, ("y", "zh"), 16).reshape(ROWS, D_T)

    exp_t, exp_s, prompts, total = teacher_score(
        pooled, scores_s, total_s, teacher_prompts, student_prompts, got
    )
    stats = spread(total, ("y", "zh"), 16)
    grad_term, place = gradient(exp_t, exp_s, total, stats, prompts)

    grad = exchange_sum(grad_term, "y", starts_y)
    others = [
        lax.ppermute(place, "zl", flip2),
        lax.ppermute(place, "xhi", flip2),
        lax.ppermute(place, ("xhi", "zl"), flip4),
    ]
    grad = exchange_sum(grad, "zh", starts_z).astype(BF16)
    patch_kl = ((place + others[0]) + others[1]) + others[2]
    grad, patch_kl = lax.optimization_barrier((grad, patch_kl))
    grad = spread(grad, "zh", 4)
    grad = spread(grad, ("xhi", "y", "zl"), 2 * n_w)
    patch_grad = grad.reshape(n_w, 2, 4, 16, D_S).transpose(2, 0, 1, 3, 4)

    return patch_kl, patch_grad.reshape(student_patches.shape)


def solution(mesh):
    split = Mesh(mesh.devices.reshape(2, 2, 2, 4, 4, 2), IMG + PRM)
    placed = (
        P(IMG, PRM, None),
        P(),
        P(IMG),
        P(PRM, None),
        P(IMG, None, None),
        P(PRM, None),
    )
    return jax.shard_map(
        body,
        mesh=split,
        in_specs=placed,
        out_specs=(P(IMG, None), P(IMG, None, None)),
        check_vma=False,
    )
```

profile of v0, /device:TPU:2, one launch (start us, length us, event | category | flops | bytes accessed | tf_op | source)
XLA Modules:
  0.0 149.7 jit_solution(4144885705184126675)
XLA Ops:
  0.6 0.0 copy-start
  0.6 0.0 copy-start.3
  0.7 0.0 copy-start.2
  0.7 1.3 half.1
  2.0 1.6 %collective-permute-start.2 = (bf16[256,1920]{1,0:T(8,128)(2,1)S(1)}, bf16[256,1920]{1,0:T(8,128)(2,1)S(1)}, u32[]{:S(2)}, u32[]{:S(2)}) collective-permute-start(bf16[256,1920]{1,0:T(8,128)(2,1)S(1)} %half.1), channel_id=1, source_target_pairs={{0,160},{32,128},{128,32},{160,0},{1,161},{33,129},{129,33},{161,1... | collective-permute-start | bytes 2949128 | tf_op jit(solution)/shard_map/ppermute | solution.py:254
  3.6 1.9 %collective-permute-start.1 = (bf16[256,1920]{1,0:T(8,128)(2,1)S(1)}, bf16[256,1920]{1,0:T(8,128)(2,1)}, u32[]{:S(2)}, u32[]{:S(2)}) collective-permute-start(bf16[256,1920]{1,0:T(8,128)(2,1)S(1)} %half.1), channel_id=1, source_target_pairs={{0,1},{1,0},{2,3},{3,2},{4,5},{5,4},{6,7},{7,6},{8,9},{9,8},{10,11... | collective-permute-start | bytes 2949128 | tf_op jit(solution)/shard_map/ppermute | solution.py:253
  5.5 0.0 copy-done.3
  5.5 0.1 iota_compare_fusion
  5.6 8.0 %all_gather.3 = bf16[16,16,1152]{2,1,0:T(8,128)(2,1)S(1)} all-gather(bf16[4,16,1152]{2,1,0:T(8,128)(2,1)} %param.6), channel_id=1, replica_groups=mesh['xlo'=2,'core'=2,'xhi'=2,'y'=4,'zh'=4,'zl'=2] {'xlo','core'}, dimensions={0}, use_global_device_ids=true | all-gather | bytes 737280 | tf_op jit(solution)/shard_map/all_gather | solution.py:275
  13.6 1.0 select_reduce_fusion
  14.6 1.3 collective-permute-start
  15.9 0.1 iota_add_fusion
  16.0 0.1 add.122
  16.1 0.0 copy-done.2
  16.1 0.1 constant_dynamic-slice_fusion.7
  16.1 0.1 convert_reduce_fusion
  16.3 0.1 broadcast_in_dim.105
  16.4 6.5 %collective-permute-done = bf16[4,16,1152]{2,1,0:T(8,128)(2,1)} collective-permute-done((bf16[4,16,1152]{2,1,0:T(8,128)(2,1)}, bf16[4,16,1152]{2,1,0:T(8,128)(2,1)}, u32[]{:S(2)}, u32[]{:S(2)}) %collective-permute-start) | collective-permute-done | bytes 147488 | tf_op jit(solution)/shard_map/ppermute | solution.py:280
  22.9 1.1 bitcast_select_fusion
  24.0 3.1 %collective-permute-done.1.refs_1_ = bf16[256,1920]{1,0:T(8,128)(2,1)} collective-permute-done((bf16[256,1920]{1,0:T(8,128)(2,1)S(1)}, bf16[256,1920]{1,0:T(8,128)(2,1)}, u32[]{:S(2)}, u32[]{:S(2)}) %collective-permute-start.1) | collective-permute-done | bytes 983072 | tf_op jit(solution)/shard_map/ppermute | solution.py:253
  27.1 0.5 collective-permute-start.3
  27.6 19.2 %all_to_all.25 = bf16[8,16,1152]{2,1,0:T(8,128)(2,1)S(1)} all-to-all(bf16[8,16,1152]{2,1,0:T(8,128)(2,1)S(1)} %bitcast_select_fusion), channel_id=1, replica_groups=mesh['xlo'=2,'core'=2,'xhi'=2,'y'=4,'zh'=4,'zl'=2] {'zh','zl'}, dimensions={0} | all-to-all | bytes 589824 | tf_op jit(solution)/shard_map/all_to_all | solution.py:24
  46.8 0.2 fusion
  46.9 0.0 collective-permute-done.2.refs_0_
  46.9 0.0 copy-start.1
  47.0 0.9 broadcast_in_dim.116
  47.9 4.6 %all-to-all-start.1 = ((bf16[16,16,1152]{2,1,0:T(8,128)(2,1)}), bf16[16,16,1152]{2,1,0:T(8,128)(2,1)S(1)}, u32[]{:S(2)}, u32[]{:S(2)}) async-start(bf16[16,16,1152]{2,1,0:T(8,128)(2,1)} %broadcast_in_dim.116), calls=%async_computation.1 | async-start | bytes 1179648 | tf_op jit(solution)/shard_map/all_to_all | solution.py:24
  52.4 0.1 collective-permute-start.5
  52.5 0.5 collective-permute-start.4
  53.0 0.0 collective-permute-done.3.refs_2_
  53.0 0.1 collective-permute-start.6
  53.2 0.8 copy.13
  54.0 1.9 %collective-permute-done.5.refs_4_ = bf16[256,1920]{1,0:T(8,128)(2,1)} collective-permute-done((bf16[256,1920]{1,0:T(8,128)(2,1)}, bf16[256,1920]{1,0:T(8,128)(2,1)}, u32[]{:S(2)}, u32[]{:S(2)}) %collective-permute-start.5) | collective-permute-done | bytes 983072 | tf_op jit(solution)/shard_map/ppermute | solution.py:294
  55.8 1.8 %collective-permute-done.4.refs_3_ = bf16[256,1920]{1,0:T(8,128)(2,1)} collective-permute-done((bf16[256,1920]{1,0:T(8,128)(2,1)S(1)}, bf16[256,1920]{1,0:T(8,128)(2,1)}, u32[]{:S(2)}, u32[]{:S(2)}) %collective-permute-start.4) | collective-permute-done | bytes 983072 | tf_op jit(solution)/shard_map/ppermute | solution.py:294
  57.7 0.6 collective-permute-done.6.refs_5_
  58.3 4.3 %student.3 = (f32[2048,256]{1,0:T(8,128)}, f32[8,256]{1,0:T(8,128)S(1)}) custom-call(bf16[256,768]{1,0:T(8,128)(2,1)} %bitcast.22, bf16[512,768]{1,0:T(8,128)(2,1)} %own_s.3, bf16[256,1920]{1,0:T(8,128)(2,1)} %copy-done.1, bf16[256,1920]{1,0:T(8,128)(2,1)} %collective-permute-done.1.refs_1_, bf16[256,1920]{1,0:T(8,128)(2,1)} %collective-permute-done.3.refs_2_, ...), custom_call_target="tpu_custom_call" | custom-call | flops 805306368 | bytes 6291456 | tf_op jit(solution)/shard_map/student/pallas_call | solution.py:102
  62.6 7.2 %all-to-all-done.1 = bf16[16,16,1152]{2,1,0:T(8,128)(2,1)S(1)} async-done(((bf16[16,16,1152]{2,1,0:T(8,128)(2,1)}), bf16[16,16,1152]{2,1,0:T(8,128)(2,1)S(1)}, u32[]{:S(2)}, u32[]{:S(2)}) %all-to-all-start.1) | async-done | bytes 589856 | tf_op jit(solution)/shard_map/all_to_all | solution.py:24
  69.8 4.7 %teacher.3 = (f32[2048,256]{1,0:T(8,128)S(1)}, f32[2048,256]{1,0:T(8,128)S(1)}, bf16[2048,768]{1,0:T(8,128)(2,1)S(1)}, f32[8,256]{1,0:T(8,128)S(1)}) custom-call(bf16[256,1152]{1,0:T(8,128)(2,1)S(1)} %bitcast.19, f32[8,256]{1,0:T(8,128)S(1)} %get-tuple-element.34.total_s, bf16[512,1152]{1,0:T(8,128)(2,1)} %own_t.1, f32[2048,256]{1,0:T(8,128)} %get-tuple-element.35.scores_s, ...), custom_call_target="tpu_custom_call" | custom-call | flops 1207959552 | bytes 14680064 | tf_op jit(solution)/shard_map/teacher/pallas_call | solution.py:176
  74.5 14.1 %all_to_all.26.stats = f32[16,8,256]{2,1,0:T(8,128)S(1)} all-to-all(f32[16,8,256]{2,1,0:T(8,128)S(1)} %broadcast_in_dim.117), channel_id=1, replica_groups=mesh['xlo'=2,'core'=2,'xhi'=2,'y'=4,'zh'=4,'zl'=2] {'y','zh'}, dimensions={0} | all-to-all | bytes 262144 | tf_op jit(solution)/shard_map/all_to_all | solution.py:24
  88.6 1.1 gradient.1
  89.7 0.1 constant_dynamic-slice_fusion.5
  89.8 0.1 collective-permute-start.7
  89.9 1.4 collective-permute-start.9
  91.3 2.7 %collective-permute-start.8 = (f32[64,768]{1,0:T(8,128)S(1)}, f32[64,768]{1,0:T(8,128)S(1)}, u32[]{:S(2)}, u32[]{:S(2)}) collective-permute-start(f32[64,768]{1,0:T(8,128)S(1)} %get-tuple-element.54), channel_id=1, source_target_pairs={{0,16},{8,24},{16,0},{24,8},{1,17},{9,25},{17,1},{25,9},{2,18},{10... | collective-permute-start | bytes 589832 | tf_op jit(solution)/shard_map/ppermute | solution.py:36
  94.0 4.1 %collective-permute-start.15 = (f32[4,256]{1,0:T(4,128)S(1)}, f32[4,256]{1,0:T(4,128)S(1)}, u32[]{:S(2)}, u32[]{:S(2)}) collective-permute-start(f32[4,256]{1,0:T(4,128)S(1)} %get-tuple-element.49), channel_id=1, source_target_pairs={{0,33},{1,32},{32,1},{33,0},{2,35},{3,34},{34,3},{35,2},{4,37},{5,... | collective-permute-start | bytes 12296 | tf_op jit(solution)/shard_map/ppermute | solution.py:308
  98.0 0.3 collective-permute-start.14
  98.3 0.0 collective-permute-done.7
  98.3 0.8 collective-permute-start.13
  99.2 0.8 collective-permute-done.9
  99.9 0.0 collective-permute-done.8
  100.0 0.2 collective-permute-start.10
  100.2 1.5 collective-permute-start.12
  101.7 0.0 collective-permute-done.15
  101.7 4.9 %collective-permute-start.11 = (f32[16,768]{1,0:T(8,128)S(1)}, f32[16,768]{1,0:T(8,128)S(1)}, u32[]{:S(2)}, u32[]{:S(2)}) collective-permute-start(f32[16,768]{1,0:T(8,128)S(1)} %get-tuple-element.57), channel_id=1, source_target_pairs={{0,4},{2,6},{4,0},{6,2},{1,5},{3,7},{5,1},{7,3},{8,12},{10,14},{12... | collective-permute-start | bytes 147464 | tf_op jit(solution)/shard_map/ppermute | solution.py:36
  106.6 0.0 collective-permute-done.14
  106.6 0.0 collective-permute-done.13
  106.6 0.6 add_add_fusion.1
  107.2 0.0 collective-permute-done.10
  107.2 0.0 collective-permute-done.12
  107.2 2.9 %collective-permute-done.11 = f32[16,768]{1,0:T(8,128)S(1)} collective-permute-done((f32[16,768]{1,0:T(8,128)S(1)}, f32[16,768]{1,0:T(8,128)S(1)}, u32[]{:S(2)}, u32[]{:S(2)}) %collective-permute-start.11) | collective-permute-done | bytes 49184 | tf_op jit(solution)/shard_map/ppermute | solution.py:36
  110.2 14.3 %all_to_all.27 = bf16[4,16,768]{2,1,0:T(8,128)(2,1)S(1)} all-to-all(bf16[4,16,768]{2,1,0:T(8,128)(2,1)S(1)} %broadcast_in_dim.118), channel_id=1, replica_groups=mesh['xlo'=2,'core'=2,'xhi'=2,'y'=4,'zh'=4,'zl'=2] {'zh'}, dimensions={0} | all-to-all | bytes 196608 | tf_op jit(solution)/shard_map/all_to_all | solution.py:24
  124.4 0.1 broadcast_in_dim.119
  124.6 23.7 %all_to_all.28 = bf16[16,4,16,768]{3,2,1,0:T(8,128)(2,1)S(1)} all-to-all(bf16[16,4,16,768]{3,2,1,0:T(8,128)(2,1)S(1)} %broadcast_in_dim.119), channel_id=1, replica_groups=mesh['xlo'=2,'core'=2,'xhi'=2,'y'=4,'zh'=4,'zl'=2] {'xhi','y','zl'}, dimensions={0} | all-to-all | bytes 3145728 | tf_op jit(solution)/shard_map/all_to_all | solution.py:24
  148.3 1.3 copy.14
  (11 shorter events, 0.2 us)
Async XLA Ops:
  0.6 52.5 %copy-start = (bf16[4,256,768]{2,1,0:T(8,128)(2,1)S(1)}, bf16[4,256,768]{2,1,0:T(8,128)(2,1)}, u32[]{:S(2)}) copy-start(bf16[4,256,768]{2,1,0:T(8,128)(2,1)} %param.10) | copy-start | bytes 4718596
  0.6 4.8 %copy-start.3 = (s32[4]{0:T(128)S(1)}, s32[4]{0:T(128)}, u32[]{:S(2)}) copy-start(s32[4]{0:T(128)} %param.8) | copy-start | bytes 52
  0.7 15.4 %copy-start.2 = (s32[256,4]{0,1:T(4,128)S(1)}, s32[256,4]{0,1:T(4,128)}, u32[]{:S(2)}) copy-start(s32[256,4]{0,1:T(4,128)} %param.7) | copy-start | bytes 12292
  2.0 45.0 %collective-permute-start.2 = (bf16[256,1920]{1,0:T(8,128)(2,1)S(1)}, bf16[256,1920]{1,0:T(8,128)(2,1)S(1)}, u32[]{:S(2)}, u32[]{:S(2)}) collective-permute-start(bf16[256,1920]{1,0:T(8,128)(2,1)S(1)} %half.1), channel_id=1, source_target_pairs={{0,160},{32,128},{128,32},{160,0},{1,161},{33,129},{129,33},{161,1... | collective-permute-start | bytes 2949128 | tf_op jit(solution)/shard_map/ppermute | solution.py:254
  3.6 23.5 %collective-permute-start.1 = (bf16[256,1920]{1,0:T(8,128)(2,1)S(1)}, bf16[256,1920]{1,0:T(8,128)(2,1)}, u32[]{:S(2)}, u32[]{:S(2)}) collective-permute-start(bf16[256,1920]{1,0:T(8,128)(2,1)S(1)} %half.1), channel_id=1, source_target_pairs={{0,1},{1,0},{2,3},{3,2},{4,5},{5,4},{6,7},{7,6},{8,9},{9,8},{10,11... | collective-permute-start | bytes 2949128 | tf_op jit(solution)/shard_map/ppermute | solution.py:253
  14.6 8.3 %collective-permute-start = (bf16[4,16,1152]{2,1,0:T(8,128)(2,1)}, bf16[4,16,1152]{2,1,0:T(8,128)(2,1)}, u32[]{:S(2)}, u32[]{:S(2)}) collective-permute-start(bf16[4,16,1152]{2,1,0:T(8,128)(2,1)} %select_reduce_fusion), channel_id=1, source_target_pairs={{8,0},{9,1},{16,8},{17,9},{24,16},{25,17},{32,24},{33,25},{40,32},... | collective-permute-start | bytes 442376 | tf_op jit(solution)/shard_map/ppermute | solution.py:280
  27.1 26.0 %collective-permute-start.3 = (bf16[256,1920]{1,0:T(8,128)(2,1)}, bf16[256,1920]{1,0:T(8,128)(2,1)}, u32[]{:S(2)}, u32[]{:S(2)}) collective-permute-start(bf16[256,1920]{1,0:T(8,128)(2,1)} %collective-permute-done.1.refs_1_), channel_id=1, source_target_pairs={{0,160},{32,128},{128,32},{160,0},{1,161},{33,129},{129,33},{161,1... | collective-permute-start | bytes 2949128 | tf_op jit(solution)/shard_map/ppermute | solution.py:287
  46.9 11.3 %copy-start.1 = (bf16[256,1920]{1,0:T(8,128)(2,1)}, bf16[256,1920]{1,0:T(8,128)(2,1)S(1)}, u32[]{:S(2)}) copy-start(bf16[256,1920]{1,0:T(8,128)(2,1)S(1)} %collective-permute-done.2.refs_0_) | copy-start | bytes 2949124
  47.9 21.9 %all-to-all-start.1 = ((bf16[16,16,1152]{2,1,0:T(8,128)(2,1)}), bf16[16,16,1152]{2,1,0:T(8,128)(2,1)S(1)}, u32[]{:S(2)}, u32[]{:S(2)}) async-start(bf16[16,16,1152]{2,1,0:T(8,128)(2,1)} %broadcast_in_dim.116), calls=%async_computation.1 | async-start | bytes 1179648 | tf_op jit(solution)/shard_map/all_to_all | solution.py:24
  52.4 3.4 %collective-permute-start.5 = (bf16[256,1920]{1,0:T(8,128)(2,1)}, bf16[256,1920]{1,0:T(8,128)(2,1)}, u32[]{:S(2)}, u32[]{:S(2)}) collective-permute-start(bf16[256,1920]{1,0:T(8,128)(2,1)} %collective-permute-done.1.refs_1_), channel_id=1, source_target_pairs={{0,64},{64,0},{1,65},{65,1},{2,66},{66,2},{3,67},{67,3},{4,68},{68... | collective-permute-start | bytes 2949128 | tf_op jit(solution)/shard_map/ppermute | solution.py:294
  52.5 5.1 %collective-permute-start.4 = (bf16[256,1920]{1,0:T(8,128)(2,1)S(1)}, bf16[256,1920]{1,0:T(8,128)(2,1)}, u32[]{:S(2)}, u32[]{:S(2)}) collective-permute-start(bf16[256,1920]{1,0:T(8,128)(2,1)S(1)} %collective-permute-done.2.refs_0_), channel_id=1, source_target_pairs={{0,64},{64,0},{1,65},{65,1},{2,66},{66,2},{3,67},{67,3},{4,68},{68... | collective-permute-start | bytes 2949128 | tf_op jit(solution)/shard_map/ppermute | solution.py:294
  53.0 5.2 %collective-permute-start.6 = (bf16[256,1920]{1,0:T(8,128)(2,1)}, bf16[256,1920]{1,0:T(8,128)(2,1)}, u32[]{:S(2)}, u32[]{:S(2)}) collective-permute-start(bf16[256,1920]{1,0:T(8,128)(2,1)} %collective-permute-done.3.refs_2_), channel_id=1, source_target_pairs={{0,64},{64,0},{1,65},{65,1},{2,66},{66,2},{3,67},{67,3},{4,68},{68... | collective-permute-start | bytes 2949128 | tf_op jit(solution)/shard_map/ppermute | solution.py:294
  89.8 8.5 %collective-permute-start.7 = (f32[64,768]{1,0:T(8,128)S(1)}, f32[64,768]{1,0:T(8,128)S(1)}, u32[]{:S(2)}, u32[]{:S(2)}) collective-permute-start(f32[64,768]{1,0:T(8,128)S(1)} %get-tuple-element.52), channel_id=1, source_target_pairs={{0,8},{8,0},{16,24},{24,16},{1,9},{9,1},{17,25},{25,17},{2,10},{10... | collective-permute-start | bytes 589832 | tf_op jit(solution)/shard_map/ppermute | solution.py:36
  89.9 10.0 %collective-permute-start.9 = (f32[64,768]{1,0:T(8,128)S(1)}, f32[64,768]{1,0:T(8,128)S(1)}, u32[]{:S(2)}, u32[]{:S(2)}) collective-permute-start(f32[64,768]{1,0:T(8,128)S(1)} %get-tuple-element.53), channel_id=1, source_target_pairs={{0,24},{8,16},{16,8},{24,0},{1,25},{9,17},{17,9},{25,1},{2,26},{10... | collective-permute-start | bytes 589832 | tf_op jit(solution)/shard_map/ppermute | solution.py:36
  91.3 8.6 %collective-permute-start.8 = (f32[64,768]{1,0:T(8,128)S(1)}, f32[64,768]{1,0:T(8,128)S(1)}, u32[]{:S(2)}, u32[]{:S(2)}) collective-permute-start(f32[64,768]{1,0:T(8,128)S(1)} %get-tuple-element.54), channel_id=1, source_target_pairs={{0,16},{8,24},{16,0},{24,8},{1,17},{9,25},{17,1},{25,9},{2,18},{10... | collective-permute-start | bytes 589832 | tf_op jit(solution)/shard_map/ppermute | solution.py:36
  94.0 7.7 %collective-permute-start.15 = (f32[4,256]{1,0:T(4,128)S(1)}, f32[4,256]{1,0:T(4,128)S(1)}, u32[]{:S(2)}, u32[]{:S(2)}) collective-permute-start(f32[4,256]{1,0:T(4,128)S(1)} %get-tuple-element.49), channel_id=1, source_target_pairs={{0,33},{1,32},{32,1},{33,0},{2,35},{3,34},{34,3},{35,2},{4,37},{5,... | collective-permute-start | bytes 12296 | tf_op jit(solution)/shard_map/ppermute | solution.py:308
  98.0 8.6 %collective-permute-start.14 = (f32[4,256]{1,0:T(4,128)S(1)}, f32[4,256]{1,0:T(4,128)S(1)}, u32[]{:S(2)}, u32[]{:S(2)}) collective-permute-start(f32[4,256]{1,0:T(4,128)S(1)} %get-tuple-element.49), channel_id=1, source_target_pairs={{0,32},{32,0},{1,33},{33,1},{2,34},{34,2},{3,35},{35,3},{4,36},{36... | collective-permute-start | bytes 12296 | tf_op jit(solution)/shard_map/ppermute | solution.py:307
  98.3 8.3 %collective-permute-start.13 = (f32[4,256]{1,0:T(4,128)S(1)}, f32[4,256]{1,0:T(4,128)S(1)}, u32[]{:S(2)}, u32[]{:S(2)}) collective-permute-start(f32[4,256]{1,0:T(4,128)S(1)} %get-tuple-element.49), channel_id=1, source_target_pairs={{0,1},{1,0},{2,3},{3,2},{4,5},{5,4},{6,7},{7,6},{8,9},{9,8},{10,11... | collective-permute-start | bytes 12296 | tf_op jit(solution)/shard_map/ppermute | solution.py:306
  100.0 7.2 %collective-permute-start.10 = (f32[16,768]{1,0:T(8,128)S(1)}, f32[16,768]{1,0:T(8,128)S(1)}, u32[]{:S(2)}, u32[]{:S(2)}) collective-permute-start(f32[16,768]{1,0:T(8,128)S(1)} %get-tuple-element.55), channel_id=1, source_target_pairs={{0,2},{2,0},{4,6},{6,4},{1,3},{3,1},{5,7},{7,5},{8,10},{10,8},{12,... | collective-permute-start | bytes 147464 | tf_op jit(solution)/shard_map/ppermute | solution.py:36
  100.2 7.0 %collective-permute-start.12 = (f32[16,768]{1,0:T(8,128)S(1)}, f32[16,768]{1,0:T(8,128)S(1)}, u32[]{:S(2)}, u32[]{:S(2)}) collective-permute-start(f32[16,768]{1,0:T(8,128)S(1)} %get-tuple-element.56), channel_id=1, source_target_pairs={{0,6},{2,4},{4,2},{6,0},{1,7},{3,5},{5,3},{7,1},{8,14},{10,12},{12... | collective-permute-start | bytes 147464 | tf_op jit(solution)/shard_map/ppermute | solution.py:36
  101.7 8.5 %collective-permute-start.11 = (f32[16,768]{1,0:T(8,128)S(1)}, f32[16,768]{1,0:T(8,128)S(1)}, u32[]{:S(2)}, u32[]{:S(2)}) collective-permute-start(f32[16,768]{1,0:T(8,128)S(1)} %get-tuple-element.57), channel_id=1, source_target_pairs={{0,4},{2,6},{4,0},{6,2},{1,5},{3,7},{5,1},{7,3},{8,12},{10,14},{12... | collective-permute-start | bytes 147464 | tf_op jit(solution)/shard_map/ppermute | solution.py:36
where the time goes:
time: 150 us
  blocking collectives  79.3 us (53%)
  starting transfers between devices  26.5 us (18%)
  waiting for transfers between devices  24.9 us (17%)
  Pallas kernels  11.4 us (8%)
  local copies, waits for them, and re-layouts  3.57 us (2%)
  other arithmetic  2.98 us (2%)
    all_to_all x4, blocking collectives, swap(): return lax.all_to_all(x, axis, split_axis=0, concat_axis=0, tiled=True)  71.3 us
    ppermute x6, starting transfers between devices, exchange_sum(): total = total + lax.ppermute(part, axis, [(i, i ^ k) for i in range(4)])  10.8 us
    all_gather x1, blocking collectives, body(): every_map = lax.all_gather(teacher_maps, IMG, axis=0, tiled=True)  8.04 us
    all_to_all x1, waiting for transfers between devices, swap(): return lax.all_to_all(x, axis, split_axis=0, concat_axis=0, tiled=True)  7.23 us
    ppermute x1, waiting for transfers between devices, body(): halo = lax.ppermute(owned, PRM, pairs)  6.54 us
    pallas_call x1, Pallas kernels, teacher_score(): pl.pallas_call(teacher_kernel, in_specs=[vmem, vmem] + [hbm] * 9, out_spe...  4.72 us
    all_to_all x1, starting transfers between devices, swap(): return lax.all_to_all(x, axis, split_axis=0, concat_axis=0, tiled=True)  4.57 us
    pallas_call x1, Pallas kernels, student_score(): pl.pallas_call(student_kernel, in_specs=[hbm] * 8, out_specs=[hbm, pl.Blo...  4.29 us
  transfers between devices with their start and end apart: 17, of which 8 were waited for; matrix products, arithmetic and copies ran while one was open for 3% of the time, Pallas kernels for 3%

commit v1 on v0

--- a/solution.py
+++ b/solution.py
@@ -31,7 +31,7 @@
 def exchange_sum(x, axis, starts):
     rows = x.shape[0] // 4
     total = lax.dynamic_slice_in_dim(x, starts[0], rows, 0, allow_negative_indices=False)
-    for k in range(1, 4):
+    for k in (2, 1, 3):
         part = lax.dynamic_slice_in_dim(x, starts[k], rows, 0, allow_negative_indices=False)
         total = total + lax.ppermute(part, axis, [(i, i ^ k) for i in range(4)])
     return total

time: 150 us -> 149 us (level)
  transfers between devices with their start and end apart: 17 -> 17, of which waited for: 8 -> 10; matrix products, arithmetic and copies ran while one was open for 3% -> 3% of each run, Pallas kernels for 3% -> 3%
where the time goes in v1:
time: 149 us; the launch traced here: 148 us
  blocking collectives  78.5 us (53%)
  starting transfers between devices  26.2 us (18%)
  waiting for transfers between devices  24.5 us (16%)
  Pallas kernels  11.4 us (8%)
  local copies, waits for them, and re-layouts  3.57 us (2%)
  other arithmetic  2.98 us (2%)
    all_to_all x4, blocking collectives, swap(): return lax.all_to_all(x, axis, split_axis=0, concat_axis=0, tiled=True)  70.5 us
    ppermute x6, starting transfers between devices, exchange_sum(): total = total + lax.ppermute(part, axis, [(i, i ^ k) for i in range(4)])  10.2 us
    all_gather x1, blocking collectives, body(): every_map = lax.all_gather(teacher_maps, IMG, axis=0, tiled=True)  8.04 us
    all_to_all x1, waiting for transfers between devices, swap(): return lax.all_to_all(x, axis, split_axis=0, concat_axis=0, tiled=True)  7.23 us
    ppermute x1, waiting for transfers between devices, body(): halo = lax.ppermute(owned, PRM, pairs)  6.54 us
    pallas_call x1, Pallas kernels, teacher_score(): pl.pallas_call(teacher_kernel, in_specs=[vmem, vmem] + [hbm] * 9, out_spe...  4.72 us
    all_to_all x1, starting transfers between devices, swap(): return lax.all_to_all(x, axis, split_axis=0, concat_axis=0, tiled=True)  4.57 us
    pallas_call x1, Pallas kernels, student_score(): pl.pallas_call(student_kernel, in_specs=[hbm] * 8, out_specs=[hbm, pl.Blo...  4.29 us
  transfers between devices with their start and end apart: 17, of which 10 were waited for; matrix products, arithmetic and copies ran while one was open for 3% of the time, Pallas kernels for 3%

profile of v1, /device:TPU:2, one launch (start us, length us, event | category | flops | bytes accessed | tf_op | source)
XLA Modules:
  0.0 148.2 jit_solution(6894776670171706212)
XLA Ops:
  0.6 0.0 copy-start
  0.6 0.0 copy-start.3
  0.7 0.0 copy-start.2
  0.7 1.3 half.1
  2.0 1.6 %collective-permute-start.2 = (bf16[256,1920]{1,0:T(8,128)(2,1)S(1)}, bf16[256,1920]{1,0:T(8,128)(2,1)S(1)}, u32[]{:S(2)}, u32[]{:S(2)}) collective-permute-start(bf16[256,1920]{1,0:T(8,128)(2,1)S(1)} %half.1), channel_id=1, source_target_pairs={{0,160},{32,128},{128,32},{160,0},{1,161},{33,129},{129,33},{161,1... | collective-permute-start | bytes 2949128 | tf_op jit(solution)/shard_map/ppermute | solution.py:254
  3.6 1.9 %collective-permute-start.1 = (bf16[256,1920]{1,0:T(8,128)(2,1)S(1)}, bf16[256,1920]{1,0:T(8,128)(2,1)}, u32[]{:S(2)}, u32[]{:S(2)}) collective-permute-start(bf16[256,1920]{1,0:T(8,128)(2,1)S(1)} %half.1), channel_id=1, source_target_pairs={{0,1},{1,0},{2,3},{3,2},{4,5},{5,4},{6,7},{7,6},{8,9},{9,8},{10,11... | collective-permute-start | bytes 2949128 | tf_op jit(solution)/shard_map/ppermute | solution.py:253
  5.5 0.0 copy-done.3
  5.5 0.1 iota_compare_fusion
  5.6 8.0 %all_gather.3 = bf16[16,16,1152]{2,1,0:T(8,128)(2,1)S(1)} all-gather(bf16[4,16,1152]{2,1,0:T(8,128)(2,1)} %param.6), channel_id=1, replica_groups=mesh['xlo'=2,'core'=2,'xhi'=2,'y'=4,'zh'=4,'zl'=2] {'xlo','core'}, dimensions={0}, use_global_device_ids=true | all-gather | bytes 737280 | tf_op jit(solution)/shard_map/all_gather | solution.py:275
  13.6 1.0 select_reduce_fusion
  14.6 1.3 collective-permute-start
  15.9 0.1 iota_add_fusion
  16.0 0.1 add.122
  16.1 0.0 copy-done.2
  16.1 0.1 constant_dynamic-slice_fusion.7
  16.1 0.1 convert_reduce_fusion
  16.3 0.1 broadcast_in_dim.105
  16.4 6.5 %collective-permute-done = bf16[4,16,1152]{2,1,0:T(8,128)(2,1)} collective-permute-done((bf16[4,16,1152]{2,1,0:T(8,128)(2,1)}, bf16[4,16,1152]{2,1,0:T(8,128)(2,1)}, u32[]{:S(2)}, u32[]{:S(2)}) %collective-permute-start) | collective-permute-done | bytes 147488 | tf_op jit(solution)/shard_map/ppermute | solution.py:280
  22.9 1.1 bitcast_select_fusion
  24.0 3.1 %collective-permute-done.1.refs_1_ = bf16[256,1920]{1,0:T(8,128)(2,1)} collective-permute-done((bf16[256,1920]{1,0:T(8,128)(2,1)S(1)}, bf16[256,1920]{1,0:T(8,128)(2,1)}, u32[]{:S(2)}, u32[]{:S(2)}) %collective-permute-start.1) | collective-permute-done | bytes 983072 | tf_op jit(solution)/shard_map/ppermute | solution.py:253
  27.1 0.5 collective-permute-start.3
  27.6 19.2 %all_to_all.25 = bf16[8,16,1152]{2,1,0:T(8,128)(2,1)S(1)} all-to-all(bf16[8,16,1152]{2,1,0:T(8,128)(2,1)S(1)} %bitcast_select_fusion), channel_id=1, replica_groups=mesh['xlo'=2,'core'=2,'xhi'=2,'y'=4,'zh'=4,'zl'=2] {'zh','zl'}, dimensions={0} | all-to-all | bytes 589824 | tf_op jit(solution)/shard_map/all_to_all | solution.py:24
  46.8 0.2 fusion
  46.9 0.0 collective-permute-done.2.refs_0_
  46.9 0.0 copy-start.1
  47.0 0.9 broadcast_in_dim.116
  47.9 4.6 %all-to-all-start.1 = ((bf16[16,16,1152]{2,1,0:T(8,128)(2,1)}), bf16[16,16,1152]{2,1,0:T(8,128)(2,1)S(1)}, u32[]{:S(2)}, u32[]{:S(2)}) async-start(bf16[16,16,1152]{2,1,0:T(8,128)(2,1)} %broadcast_in_dim.116), calls=%async_computation.1 | async-start | bytes 1179648 | tf_op jit(solution)/shard_map/all_to_all | solution.py:24
  52.4 0.1 collective-permute-start.5
  52.5 0.5 collective-permute-start.4
  53.0 0.0 collective-permute-done.3.refs_2_
  53.0 0.1 collective-permute-start.6
  53.2 0.8 copy.13
  54.0 1.9 %collective-permute-done.5.refs_4_ = bf16[256,1920]{1,0:T(8,128)(2,1)} collective-permute-done((bf16[256,1920]{1,0:T(8,128)(2,1)}, bf16[256,1920]{1,0:T(8,128)(2,1)}, u32[]{:S(2)}, u32[]{:S(2)}) %collective-permute-start.5) | collective-permute-done | bytes 983072 | tf_op jit(solution)/shard_map/ppermute | solution.py:294
  55.8 1.8 %collective-permute-done.4.refs_3_ = bf16[256,1920]{1,0:T(8,128)(2,1)} collective-permute-done((bf16[256,1920]{1,0:T(8,128)(2,1)S(1)}, bf16[256,1920]{1,0:T(8,128)(2,1)}, u32[]{:S(2)}, u32[]{:S(2)}) %collective-permute-start.4) | collective-permute-done | bytes 983072 | tf_op jit(solution)/shard_map/ppermute | solution.py:294
  57.7 0.6 collective-permute-done.6.refs_5_
  58.3 4.3 %student.3 = (f32[2048,256]{1,0:T(8,128)}, f32[8,256]{1,0:T(8,128)S(1)}) custom-call(bf16[256,768]{1,0:T(8,128)(2,1)} %bitcast.22, bf16[512,768]{1,0:T(8,128)(2,1)} %own_s.3, bf16[256,1920]{1,0:T(8,128)(2,1)} %copy-done.1, bf16[256,1920]{1,0:T(8,128)(2,1)} %collective-permute-done.1.refs_1_, bf16[256,1920]{1,0:T(8,128)(2,1)} %collective-permute-done.3.refs_2_, ...), custom_call_target="tpu_custom_call" | custom-call | flops 805306368 | bytes 6291456 | tf_op jit(solution)/shard_map/student/pallas_call | solution.py:102
  62.6 7.2 %all-to-all-done.1 = bf16[16,16,1152]{2,1,0:T(8,128)(2,1)S(1)} async-done(((bf16[16,16,1152]{2,1,0:T(8,128)(2,1)}), bf16[16,16,1152]{2,1,0:T(8,128)(2,1)S(1)}, u32[]{:S(2)}, u32[]{:S(2)}) %all-to-all-start.1) | async-done | bytes 589856 | tf_op jit(solution)/shard_map/all_to_all | solution.py:24
  69.8 4.7 %teacher.3 = (f32[2048,256]{1,0:T(8,128)S(1)}, f32[2048,256]{1,0:T(8,128)S(1)}, bf16[2048,768]{1,0:T(8,128)(2,1)S(1)}, f32[8,256]{1,0:T(8,128)S(1)}) custom-call(bf16[256,1152]{1,0:T(8,128)(2,1)S(1)} %bitcast.19, f32[8,256]{1,0:T(8,128)S(1)} %get-tuple-element.34.total_s, bf16[512,1152]{1,0:T(8,128)(2,1)} %own_t.1, f32[2048,256]{1,0:T(8,128)} %get-tuple-element.35.scores_s, ...), custom_call_target="tpu_custom_call" | custom-call | flops 1207959552 | bytes 14680064 | tf_op jit(solution)/shard_map/teacher/pallas_call | solution.py:176
  74.5 14.1 %all_to_all.26.stats = f32[16,8,256]{2,1,0:T(8,128)S(1)} all-to-all(f32[16,8,256]{2,1,0:T(8,128)S(1)} %broadcast_in_dim.117), channel_id=1, replica_groups=mesh['xlo'=2,'core'=2,'xhi'=2,'y'=4,'zh'=4,'zl'=2] {'y','zh'}, dimensions={0} | all-to-all | bytes 262144 | tf_op jit(solution)/shard_map/all_to_all | solution.py:24
  88.6 1.1 gradient.1
  89.7 0.1 constant_dynamic-slice_fusion.5
  89.8 0.9 collective-permute-start.7
  90.7 1.6 %collective-permute-start.9 = (f32[64,768]{1,0:T(8,128)S(1)}, f32[64,768]{1,0:T(8,128)S(1)}, u32[]{:S(2)}, u32[]{:S(2)}) collective-permute-start(f32[64,768]{1,0:T(8,128)S(1)} %get-tuple-element.53), channel_id=1, source_target_pairs={{0,24},{8,16},{16,8},{24,0},{1,25},{9,17},{17,9},{25,1},{2,26},{10... | collective-permute-start | bytes 589832 | tf_op jit(solution)/shard_map/ppermute | solution.py:36
  92.3 1.1 collective-permute-start.8
  93.4 4.1 %collective-permute-start.15 = (f32[4,256]{1,0:T(4,128)S(1)}, f32[4,256]{1,0:T(4,128)S(1)}, u32[]{:S(2)}, u32[]{:S(2)}) collective-permute-start(f32[4,256]{1,0:T(4,128)S(1)} %get-tuple-element.49), channel_id=1, source_target_pairs={{0,33},{1,32},{32,1},{33,0},{2,35},{3,34},{34,3},{35,2},{4,37},{5,... | collective-permute-start | bytes 12296 | tf_op jit(solution)/shard_map/ppermute | solution.py:308
  97.4 0.3 collective-permute-start.14
  97.7 0.4 collective-permute-done.7
  98.2 1.2 collective-permute-start.13
  99.3 0.8 collective-permute-done.9
  100.1 0.0 collective-permute-done.8
  100.2 0.9 collective-permute-start.10
  101.1 2.9 %collective-permute-start.12 = (f32[16,768]{1,0:T(8,128)S(1)}, f32[16,768]{1,0:T(8,128)S(1)}, u32[]{:S(2)}, u32[]{:S(2)}) collective-permute-start(f32[16,768]{1,0:T(8,128)S(1)} %get-tuple-element.56), channel_id=1, source_target_pairs={{0,6},{2,4},{4,2},{6,0},{1,7},{3,5},{5,3},{7,1},{8,14},{10,12},{12... | collective-permute-start | bytes 147464 | tf_op jit(solution)/shard_map/ppermute | solution.py:36
  104.0 0.0 collective-permute-done.15
  104.0 2.8 %collective-permute-start.11 = (f32[16,768]{1,0:T(8,128)S(1)}, f32[16,768]{1,0:T(8,128)S(1)}, u32[]{:S(2)}, u32[]{:S(2)}) collective-permute-start(f32[16,768]{1,0:T(8,128)S(1)} %get-tuple-element.57), channel_id=1, source_target_pairs={{0,2},{2,0},{4,6},{6,4},{1,3},{3,1},{5,7},{7,5},{8,10},{10,8},{12,... | collective-permute-start | bytes 147464 | tf_op jit(solution)/shard_map/ppermute | solution.py:36
  106.8 0.0 collective-permute-done.14
  106.8 0.0 collective-permute-done.13
  106.8 0.6 add_add_fusion.1
  107.4 1.4 collective-permute-done.10
  108.8 0.0 collective-permute-done.12
  108.8 0.7 collective-permute-done.11
  109.5 12.9 %all_to_all.27 = bf16[4,16,768]{2,1,0:T(8,128)(2,1)S(1)} all-to-all(bf16[4,16,768]{2,1,0:T(8,128)(2,1)S(1)} %broadcast_in_dim.118), channel_id=1, replica_groups=mesh['xlo'=2,'core'=2,'xhi'=2,'y'=4,'zh'=4,'zl'=2] {'zh'}, dimensions={0} | all-to-all | bytes 196608 | tf_op jit(solution)/shard_map/all_to_all | solution.py:24
  122.4 0.1 broadcast_in_dim.119
  122.5 24.4 %all_to_all.28 = bf16[16,4,16,768]{3,2,1,0:T(8,128)(2,1)S(1)} all-to-all(bf16[16,4,16,768]{3,2,1,0:T(8,128)(2,1)S(1)} %broadcast_in_dim.119), channel_id=1, replica_groups=mesh['xlo'=2,'core'=2,'xhi'=2,'y'=4,'zh'=4,'zl'=2] {'xhi','y','zl'}, dimensions={0} | all-to-all | bytes 3145728 | tf_op jit(solution)/shard_map/all_to_all | solution.py:24
  146.9 1.3 copy.14
  (11 shorter events, 0.2 us)
Async XLA Ops:
  0.6 52.5 %copy-start = (bf16[4,256,768]{2,1,0:T(8,128)(2,1)S(1)}, bf16[4,256,768]{2,1,0:T(8,128)(2,1)}, u32[]{:S(2)}) copy-start(bf16[4,256,768]{2,1,0:T(8,128)(2,1)} %param.10) | copy-start | bytes 4718596
  0.6 4.8 %copy-start.3 = (s32[4]{0:T(128)S(1)}, s32[4]{0:T(128)}, u32[]{:S(2)}) copy-start(s32[4]{0:T(128)} %param.8) | copy-start | bytes 52
  0.7 15.4 %copy-start.2 = (s32[256,4]{0,1:T(4,128)S(1)}, s32[256,4]{0,1:T(4,128)}, u32[]{:S(2)}) copy-start(s32[256,4]{0,1:T(4,128)} %param.7) | copy-start | bytes 12292
  2.0 45.0 %collective-permute-start.2 = (bf16[256,1920]{1,0:T(8,128)(2,1)S(1)}, bf16[256,1920]{1,0:T(8,128)(2,1)S(1)}, u32[]{:S(2)}, u32[]{:S(2)}) collective-permute-start(bf16[256,1920]{1,0:T(8,128)(2,1)S(1)} %half.1), channel_id=1, source_target_pairs={{0,160},{32,128},{128,32},{160,0},{1,161},{33,129},{129,33},{161,1... | collective-permute-start | bytes 2949128 | tf_op jit(solution)/shard_map/ppermute | solution.py:254
  3.6 23.5 %collective-permute-start.1 = (bf16[256,1920]{1,0:T(8,128)(2,1)S(1)}, bf16[256,1920]{1,0:T(8,128)(2,1)}, u32[]{:S(2)}, u32[]{:S(2)}) collective-permute-start(bf16[256,1920]{1,0:T(8,128)(2,1)S(1)} %half.1), channel_id=1, source_target_pairs={{0,1},{1,0},{2,3},{3,2},{4,5},{5,4},{6,7},{7,6},{8,9},{9,8},{10,11... | collective-permute-start | bytes 2949128 | tf_op jit(solution)/shard_map/ppermute | solution.py:253
  14.6 8.3 %collective-permute-start = (bf16[4,16,1152]{2,1,0:T(8,128)(2,1)}, bf16[4,16,1152]{2,1,0:T(8,128)(2,1)}, u32[]{:S(2)}, u32[]{:S(2)}) collective-permute-start(bf16[4,16,1152]{2,1,0:T(8,128)(2,1)} %select_reduce_fusion), channel_id=1, source_target_pairs={{8,0},{9,1},{16,8},{17,9},{24,16},{25,17},{32,24},{33,25},{40,32},... | collective-permute-start | bytes 442376 | tf_op jit(solution)/shard_map/ppermute | solution.py:280
  27.1 26.0 %collective-permute-start.3 = (bf16[256,1920]{1,0:T(8,128)(2,1)}, bf16[256,1920]{1,0:T(8,128)(2,1)}, u32[]{:S(2)}, u32[]{:S(2)}) collective-permute-start(bf16[256,1920]{1,0:T(8,128)(2,1)} %collective-permute-done.1.refs_1_), channel_id=1, source_target_pairs={{0,160},{32,128},{128,32},{160,0},{1,161},{33,129},{129,33},{161,1... | collective-permute-start | bytes 2949128 | tf_op jit(solution)/shard_map/ppermute | solution.py:287
  46.9 11.3 %copy-start.1 = (bf16[256,1920]{1,0:T(8,128)(2,1)}, bf16[256,1920]{1,0:T(8,128)(2,1)S(1)}, u32[]{:S(2)}) copy-start(bf16[256,1920]{1,0:T(8,128)(2,1)S(1)} %collective-permute-done.2.refs_0_) | copy-start | bytes 2949124
  47.9 21.9 %all-to-all-start.1 = ((bf16[16,16,1152]{2,1,0:T(8,128)(2,1)}), bf16[16,16,1152]{2,1,0:T(8,128)(2,1)S(1)}, u32[]{:S(2)}, u32[]{:S(2)}) async-start(bf16[16,16,1152]{2,1,0:T(8,128)(2,1)} %broadcast_in_dim.116), calls=%async_computation.1 | async-start | bytes 1179648 | tf_op jit(solution)/shard_map/all_to_all | solution.py:24
  52.4 3.4 %collective-permute-start.5 = (bf16[256,1920]{1,0:T(8,128)(2,1)}, bf16[256,1920]{1,0:T(8,128)(2,1)}, u32[]{:S(2)}, u32[]{:S(2)}) collective-permute-start(bf16[256,1920]{1,0:T(8,128)(2,1)} %collective-permute-done.1.refs_1_), channel_id=1, source_target_pairs={{0,64},{64,0},{1,65},{65,1},{2,66},{66,2},{3,67},{67,3},{4,68},{68... | collective-permute-start | bytes 2949128 | tf_op jit(solution)/shard_map/ppermute | solution.py:294
  52.5 5.1 %collective-permute-start.4 = (bf16[256,1920]{1,0:T(8,128)(2,1)S(1)}, bf16[256,1920]{1,0:T(8,128)(2,1)}, u32[]{:S(2)}, u32[]{:S(2)}) collective-permute-start(bf16[256,1920]{1,0:T(8,128)(2,1)S(1)} %collective-permute-done.2.refs_0_), channel_id=1, source_target_pairs={{0,64},{64,0},{1,65},{65,1},{2,66},{66,2},{3,67},{67,3},{4,68},{68... | collective-permute-start | bytes 2949128 | tf_op jit(solution)/shard_map/ppermute | solution.py:294
  53.0 5.2 %collective-permute-start.6 = (bf16[256,1920]{1,0:T(8,128)(2,1)}, bf16[256,1920]{1,0:T(8,128)(2,1)}, u32[]{:S(2)}, u32[]{:S(2)}) collective-permute-start(bf16[256,1920]{1,0:T(8,128)(2,1)} %collective-permute-done.3.refs_2_), channel_id=1, source_target_pairs={{0,64},{64,0},{1,65},{65,1},{2,66},{66,2},{3,67},{67,3},{4,68},{68... | collective-permute-start | bytes 2949128 | tf_op jit(solution)/shard_map/ppermute | solution.py:294
  89.8 8.4 %collective-permute-start.7 = (f32[64,768]{1,0:T(8,128)S(1)}, f32[64,768]{1,0:T(8,128)S(1)}, u32[]{:S(2)}, u32[]{:S(2)}) collective-permute-start(f32[64,768]{1,0:T(8,128)S(1)} %get-tuple-element.52), channel_id=1, source_target_pairs={{0,16},{8,24},{16,0},{24,8},{1,17},{9,25},{17,1},{25,9},{2,18},{10... | collective-permute-start | bytes 589832 | tf_op jit(solution)/shard_map/ppermute | solution.py:36
  90.7 9.4 %collective-permute-start.9 = (f32[64,768]{1,0:T(8,128)S(1)}, f32[64,768]{1,0:T(8,128)S(1)}, u32[]{:S(2)}, u32[]{:S(2)}) collective-permute-start(f32[64,768]{1,0:T(8,128)S(1)} %get-tuple-element.53), channel_id=1, source_target_pairs={{0,24},{8,16},{16,8},{24,0},{1,25},{9,17},{17,9},{25,1},{2,26},{10... | collective-permute-start | bytes 589832 | tf_op jit(solution)/shard_map/ppermute | solution.py:36
  92.3 7.8 %collective-permute-start.8 = (f32[64,768]{1,0:T(8,128)S(1)}, f32[64,768]{1,0:T(8,128)S(1)}, u32[]{:S(2)}, u32[]{:S(2)}) collective-permute-start(f32[64,768]{1,0:T(8,128)S(1)} %get-tuple-element.54), channel_id=1, source_target_pairs={{0,8},{8,0},{16,24},{24,16},{1,9},{9,1},{17,25},{25,17},{2,10},{10... | collective-permute-start | bytes 589832 | tf_op jit(solution)/shard_map/ppermute | solution.py:36
  93.4 10.6 %collective-permute-start.15 = (f32[4,256]{1,0:T(4,128)S(1)}, f32[4,256]{1,0:T(4,128)S(1)}, u32[]{:S(2)}, u32[]{:S(2)}) collective-permute-start(f32[4,256]{1,0:T(4,128)S(1)} %get-tuple-element.49), channel_id=1, source_target_pairs={{0,33},{1,32},{32,1},{33,0},{2,35},{3,34},{34,3},{35,2},{4,37},{5,... | collective-permute-start | bytes 12296 | tf_op jit(solution)/shard_map/ppermute | solution.py:308
  97.4 9.4 %collective-permute-start.14 = (f32[4,256]{1,0:T(4,128)S(1)}, f32[4,256]{1,0:T(4,128)S(1)}, u32[]{:S(2)}, u32[]{:S(2)}) collective-permute-start(f32[4,256]{1,0:T(4,128)S(1)} %get-tuple-element.49), channel_id=1, source_target_pairs={{0,32},{32,0},{1,33},{33,1},{2,34},{34,2},{3,35},{35,3},{4,36},{36... | collective-permute-start | bytes 12296 | tf_op jit(solution)/shard_map/ppermute | solution.py:307
  98.2 8.7 %collective-permute-start.13 = (f32[4,256]{1,0:T(4,128)S(1)}, f32[4,256]{1,0:T(4,128)S(1)}, u32[]{:S(2)}, u32[]{:S(2)}) collective-permute-start(f32[4,256]{1,0:T(4,128)S(1)} %get-tuple-element.49), channel_id=1, source_target_pairs={{0,1},{1,0},{2,3},{3,2},{4,5},{5,4},{6,7},{7,6},{8,9},{9,8},{10,11... | collective-permute-start | bytes 12296 | tf_op jit(solution)/shard_map/ppermute | solution.py:306
  100.2 8.6 %collective-permute-start.10 = (f32[16,768]{1,0:T(8,128)S(1)}, f32[16,768]{1,0:T(8,128)S(1)}, u32[]{:S(2)}, u32[]{:S(2)}) collective-permute-start(f32[16,768]{1,0:T(8,128)S(1)} %get-tuple-element.55), channel_id=1, source_target_pairs={{0,4},{2,6},{4,0},{6,2},{1,5},{3,7},{5,1},{7,3},{8,12},{10,14},{12... | collective-permute-start | bytes 147464 | tf_op jit(solution)/shard_map/ppermute | solution.py:36
  101.1 7.7 %collective-permute-start.12 = (f32[16,768]{1,0:T(8,128)S(1)}, f32[16,768]{1,0:T(8,128)S(1)}, u32[]{:S(2)}, u32[]{:S(2)}) collective-permute-start(f32[16,768]{1,0:T(8,128)S(1)} %get-tuple-element.56), channel_id=1, source_target_pairs={{0,6},{2,4},{4,2},{6,0},{1,7},{3,5},{5,3},{7,1},{8,14},{10,12},{12... | collective-permute-start | bytes 147464 | tf_op jit(solution)/shard_map/ppermute | solution.py:36
  104.0 5.5 %collective-permute-start.11 = (f32[16,768]{1,0:T(8,128)S(1)}, f32[16,768]{1,0:T(8,128)S(1)}, u32[]{:S(2)}, u32[]{:S(2)}) collective-permute-start(f32[16,768]{1,0:T(8,128)S(1)} %get-tuple-element.57), channel_id=1, source_target_pairs={{0,2},{2,0},{4,6},{6,4},{1,3},{3,1},{5,7},{7,5},{8,10},{10,8},{12,... | collective-permute-start | bytes 147464 | tf_op jit(solution)/shard_map/ppermute | solution.py:36
